TPU v7x, 32 devices: a whole 2x2x4 slice. The times are simulated.
32 devices in a mesh: seq: 8 (over z, x), head: 4 (over y, core).
Axes of the slice: x: 2, y: 2, z: 4, core: 2. Of those that a mesh axis runs over, the one named last changes fastest.
Arguments:
- ssm_input: float32 [4096, 4096], P('seq', 'head'), may hold values from -50 to 50
- gate_input: bfloat16 [4096, 4096], P('seq', 'head'), may hold values from -6 to 6
- step_raw: float32 [4096, 64], P('seq', 'head'), may hold values from -6 to 8192
- decay_log: float32 [64], P('head')
- state_in: float32 [4096, 4, 128], P('seq', 'head'), may hold values from -0.5 to 0.5
- state_out: float32 [4096, 4, 128], P('seq', 'head'), may hold values from -6 to 6
- skip_gain: float32 [64], P('head'), may hold values from 0.5 to 2
- norm_gain: float32 [4096], P('head'), may hold values from 0.25 to 1.75
- out_weight: bfloat16 [4096, 4096], P('head'), may hold values from -0.09375 to 0.09375
Outputs:
- layer_out: bfloat16 [4096, 4096], P(('seq', 'head'))
All inputs are finite; a program needn't handle non-finite values.
Results may differ from a plain program's by a relative error of at most 0.015.
Values may be sent and summed in bfloat16 or wider, within the bound.
No kernel may reach another device: no remote copies, remote signals or barrier semaphores. Data moves between devices by JAX's collectives and lax.ppermute only.
A program may use at most 192 MiB of HBM per device.

v0:
```python
import functools

import jax
import jax.numpy as jnp
from jax import lax
from jax.experimental import pallas as pl
from jax.experimental.pallas import tpu as pltpu
from jax.sharding import PartitionSpec as P

P_SIZE = 64
N = 128
CHUNK = 128
LANES = 128
BF = jnp.bfloat16
F32 = jnp.float32
VMEM_LIMIT = 24 * 1024 * 1024
WHOLE_VMEM = 60 * 1024 * 1024
PIECES = ((0, 1024), (1024, 1024), (2048, 2048))


def dot(a, b, contract=((1,), (0,)), precision=None):
    return lax.dot_general(a, b, (contract, ((), ())), precision=precision, preferred_element_type=F32)


def split2(v):
    hi = v.astype(BF)
    return hi, (v - hi.astype(F32)).astype(BF)


def split3(v):
    hi, rest = v.astype(BF), v
    rest = v - hi.astype(F32)
    mid = rest.astype(BF)
    return hi, mid, (rest - mid.astype(F32)).astype(BF)


def pick(rows, lanes, heads, per_head, first):
    r = lax.broadcasted_iota(jnp.int32, (rows, lanes), 0) % heads
    l = lax.broadcasted_iota(jnp.int32, (rows, lanes), 1) // per_head + first
    return jnp.where(r == l, 1.0, 0.0).astype(BF)


def state_kernel(raw_ref, rate_ref, x_ref, b_ref, msg_ref, aux_ref, wk):
    g = pl.program_id(0)
    heads, tok = raw_ref.shape
    width = x_ref.shape[1]
    chunks = tok // CHUNK

    @pl.when(g == 0)
    def _():
        raw = raw_ref[...]
        step = jnp.maximum(raw, 0.0) + jnp.log1p(jnp.exp(-jnp.abs(raw)))
        r = lax.broadcasted_iota(jnp.int32, (heads, heads), 0)
        l = lax.broadcasted_iota(jnp.int32, (heads, heads), 1)
        rate = jnp.sum(jnp.where(r == l, rate_ref[...], 0.0), axis=1, keepdims=True)
        logs = -step * jnp.exp(rate)
        parts = split3(logs)
        stacked = jnp.concatenate(
            [p[:, c * CHUNK:(c + 1) * CHUNK] for c in range(chunks) for p in parts], axis=0
        )
        s = lax.broadcasted_iota(jnp.int32, (CHUNK, 2 * CHUNK), 0)
        t = lax.broadcasted_iota(jnp.int32, (CHUNK, 2 * CHUNK), 1)
        tri = jnp.where(jnp.where(t < CHUNK, t - s, s - t + (CHUNK - 1)) >= 0, 1.0, 0.0).astype(BF)
        sums = dot(stacked, tri)
        pre, suf = [], []
        for c in range(chunks):
            base = 3 * heads * c
            total = (
                sums[base:base + heads] + sums[base + heads:base + 2 * heads]
            ) + sums[base + 2 * heads:base + 3 * heads]
            pre.append(total[:, :CHUNK])
            suf.append(total[:, CHUNK:])
        after = jnp.zeros((heads, 1), F32)
        for c in reversed(range(chunks)):
            w = step[:, c * CHUNK:(c + 1) * CHUNK] * jnp.exp(suf[c] + after)
            hi, lo = split2(w)
            wk[:heads, c * CHUNK:(c + 1) * CHUNK] = hi
            wk[heads:, c * CHUNK:(c + 1) * CHUNK] = lo
            after = after + pre[c][:, CHUNK - 1:]
        hi, lo = split2(jnp.broadcast_to(jnp.exp(after), (heads, CHUNK)))
        wk[:heads, tok:] = hi
        wk[heads:, tok:] = lo
        aux_ref[:heads] = step
        aux_ref[heads:2 * heads] = jnp.concatenate(pre, axis=1)
        aux_ref[2 * heads:] = jnp.concatenate(suf, axis=1)

    spread = dot(
        wk[...], pick(2 * heads, width, heads, P_SIZE, g * (width // P_SIZE)), ((0,), (0,))
    )
    weighted = (x_ref[...] * spread[:tok]).astype(BF)
    state = dot(b_ref[...].astype(BF), weighted, ((0,), (0,)))
    hi, lo = split2(spread[tok:tok + 8])
    decay = jnp.concatenate([hi.astype(F32), lo.astype(F32)], axis=0).astype(BF)
    for i in range(width // LANES):
        cut = slice(i * LANES, (i + 1) * LANES)
        msg_ref[i, :N] = state[:, cut].astype(BF)
        msg_ref[i, N:] = decay[:, cut]


def local_states(raw, rate, x, b):
    heads, tok = raw.shape
    width = 256
    blocks = x.shape[1] // LANES
    return pl.pallas_call(
        state_kernel,
        grid=(x.shape[1] // width,),
        in_specs=[
            pl.BlockSpec((heads, tok), lambda g: (0, 0)),
            pl.BlockSpec((1, heads), lambda g: (0, 0)),
            pl.BlockSpec((tok, width), lambda g: (0, g)),
            pl.BlockSpec((tok, N), lambda g: (0, 0)),
        ],
        out_specs=[
            pl.BlockSpec((width // LANES, N + 16, LANES), lambda g: (g, 0, 0)),
            pl.BlockSpec((3 * heads, tok), lambda g: (0, 0)),
        ],
        out_shape=[
            jax.ShapeDtypeStruct((blocks, N + 16, LANES), BF),
            jax.ShapeDtypeStruct((3 * heads, tok), F32),
        ],
        scratch_shapes=[pltpu.VMEM((2 * heads, tok + CHUNK), BF)],
        compiler_params=pltpu.CompilerParams(vmem_limit_bytes=WHOLE_VMEM),
        cost_estimate=pl.CostEstimate(flops=400_000_000, bytes_accessed=2_800_000, transcendentals=0),
        name="local_states",
    )(raw, rate, x, b)


def prefix_kernel(msg_ref, out_ref):
    total = jnp.zeros((N, LANES), F32)
    for j in range(msg_ref.shape[0]):
        out_ref[j] = total.astype(BF)
        tail = msg_ref[j, N:].astype(F32)
        decay = tail[:1] + tail[8:9]
        total = total * decay + msg_ref[j, :N].astype(F32)


def prefix(msg):
    count = msg.shape[0]
    return pl.pallas_call(
        prefix_kernel,
        out_shape=jax.ShapeDtypeStruct((count, N, LANES), BF),
        compiler_params=pltpu.CompilerParams(vmem_limit_bytes=VMEM_LIMIT),
        cost_estimate=pl.CostEstimate(flops=1_000_000, bytes_accessed=600_000, transcendentals=0),
        name="prefix",
    )(msg)


def within_kernel(aux_ref, x_ref, b_ref, c_ref, gate_ref, skip_ref, own_ref, lead_ref, scores, trip, duo, lines):
    g = pl.program_id(0)
    tok, width = x_ref.shape
    heads = aux_ref.shape[0] // 3
    chunks = tok // CHUNK
    here = width // P_SIZE

    @pl.when(g == 0)
    def _():
        before = jnp.zeros((heads, 1), F32)
        i = lax.broadcasted_iota(jnp.int32, (CHUNK, CHUNK), 0)
        j = lax.broadcasted_iota(jnp.int32, (CHUNK, CHUNK), 1)
        for c in range(chunks):
            cut = slice(c * CHUNK, (c + 1) * CHUNK)
            step, pre, suf = (aux_ref[k * heads:(k + 1) * heads, cut] for k in range(3))
            trip[c] = jnp.concatenate([v for v in split3(pre)], axis=0)
            for k, value in enumerate(
                (step, step * jnp.exp(suf), jnp.exp(pre), jnp.exp(pre + before))
            ):
                hi, lo = split2(value)
                duo[c, :heads, k * CHUNK:(k + 1) * CHUNK] = hi
                duo[c, heads:, k * CHUNK:(k + 1) * CHUNK] = lo
            before = before + pre[:, CHUNK - 1:]
            for k in range(heads // here):
                lines[k, :here, cut] = pre[k * here:(k + 1) * here]
            raw = dot(c_ref[cut], b_ref[cut], ((1,), (1,)), lax.Precision.HIGHEST)
            scores[c] = jnp.where(i >= j, raw, 0.0)

    spread = pick(2 * heads, width, heads, P_SIZE, g * here)
    columns = pick(3 * heads, here * CHUNK, heads, CHUNK, g * here)
    lane = lax.broadcasted_iota(jnp.int32, (CHUNK, LANES), 1)
    state = jnp.zeros((N, width), F32)
    mine = lines[g]
    for c in range(chunks):
        cut = slice(c * CHUNK, (c + 1) * CHUNK)
        wide = dot(duo[c], spread, ((0,), (0,)))
        x = x_ref[cut]
        stepped = x * wide[:CHUNK]
        lead = wide[2 * CHUNK:3 * CHUNK]
        tall = dot(trip[c], columns, ((0,), (0,)))
        outs = []
        for pair in range(here // 2):
            mixes = []
            for h in (2 * pair, 2 * pair + 1):
                gap = tall[:, h * CHUNK:(h + 1) * CHUNK] - mine[h:h + 1, cut]
                mixes.append((scores[c] * jnp.exp(jnp.minimum(gap, 0.0))).astype(BF))
            both = stepped[:, pair * LANES:(pair + 1) * LANES]
            stacked = jnp.concatenate(
                [
                    jnp.where(lane < P_SIZE, both, 0.0).astype(BF),
                    jnp.where(lane < P_SIZE, 0.0, both).astype(BF),
                ],
                axis=0,
            )
            outs.append(dot(jnp.concatenate(mixes, axis=1), stacked))
        y = jnp.concatenate(outs, axis=1) + skip_ref[...] * x
        if c:
            y = y + lead * dot(c_ref[cut].astype(BF), state.astype(BF))
        v = gate_ref[cut].astype(F32)
        silu = v / (1.0 + jnp.exp(-v))
        own_ref[cut] = y * silu
        lead_ref[cut] = wide[3 * CHUNK:] * silu
        if c < chunks - 1:
            weighted = (x * wide[CHUNK:2 * CHUNK]).astype(BF)
            added = dot(b_ref[cut].astype(BF), weighted, ((0,), (0,)))
            state = state * lead[CHUNK - 1:] + added


def within(aux, x, b, c, gate, skip):
    tok, channels = x.shape
    heads = aux.shape[0] // 3
    width = 256
    chunks = tok // CHUNK
    return pl.pallas_call(
        within_kernel,
        grid=(channels // width,),
        in_specs=[
            pl.BlockSpec((3 * heads, tok), lambda g: (0, 0)),
            pl.BlockSpec((tok, width), lambda g: (0, g)),
            pl.BlockSpec((tok, N), lambda g: (0, 0)),
            pl.BlockSpec((tok, N), lambda g: (0, 0)),
            pl.BlockSpec((tok, width), lambda g: (0, g)),
            pl.BlockSpec((1, width), lambda g: (0, g)),
        ],
        out_specs=[pl.BlockSpec((tok, width), lambda g: (0, g))] * 2,
        out_shape=[jax.ShapeDtypeStruct((tok, channels), F32)] * 2,
        scratch_shapes=[
            pltpu.VMEM((chunks, CHUNK, CHUNK), F32),
            pltpu.VMEM((chunks, 3 * heads, CHUNK), BF),
            pltpu.VMEM((chunks, 2 * heads, 4 * CHUNK), BF),
            pltpu.VMEM((channels // width, 8, tok), F32),
        ],
        compiler_params=pltpu.CompilerParams(vmem_limit_bytes=VMEM_LIMIT),
        cost_estimate=pl.CostEstimate(
            flops=2_000_000_000, bytes_accessed=5_000_000, transcendentals=1_000_000
        ),
        name="within",
    )(aux, x, b, c, gate, skip)


def finish_rows(own, lead, c, incoming_ref, gain):
    c = c.astype(BF)
    carried = jnp.concatenate([dot(c, incoming_ref[k]) for k in range(incoming_ref.shape[0])], axis=1)
    gated = own + lead * carried
    mean = jnp.mean(gated * gated, axis=1, keepdims=True)
    return (gated * lax.rsqrt(mean + 1e-05) * gain).astype(BF)


def far_kernel(
    order, o0, o1, l0, l1, c0, c1, incoming, gain, w, theirs, mine, normed, weights, sem
):
    columns = theirs.shape[1]
    rows = o0.shape[0]
    load = pltpu.make_async_copy(w.at[:, :columns], weights, sem)
    load.start()
    normed[:rows] = finish_rows(o0[...], l0[...], c0[...], incoming, gain[...])
    normed[rows:] = finish_rows(o1[...], l1[...], c1[...], incoming, gain[...])
    load.wait()
    out = dot(normed[...], weights[...])
    theirs[...] = out[:rows].astype(BF)
    mine[...] = out[rows:]


def near_kernel(order, o0, o1, l0, l1, c0, c1, incoming, gain, w, theirs, mine, normed):
    rows = o0.shape[0]

    @pl.when(pl.program_id(0) == 0)
    def _():
        normed[:rows] = finish_rows(o0[...], l0[...], c0[...], incoming, gain[...])
        normed[rows:] = finish_rows(o1[...], l1[...], c1[...], incoming, gain[...])

    out = dot(normed[...], w[...])
    theirs[...] = out[:rows].astype(BF)
    mine[...] = out[rows:]


def finish_project(order, far, own, lead, c, incoming, gain, w, columns):
    channels = own.shape[1]
    rows = CHUNK
    first = 0 if far else 2
    wide = columns if far else 1024

    def row(k):
        return lambda j, order: (order[first + k], 0)

    normed = pltpu.VMEM((2 * rows, channels), BF)
    return pl.pallas_call(
        far_kernel if far else near_kernel,
        grid_spec=pltpu.PrefetchScalarGridSpec(
            num_scalar_prefetch=1,
            grid=(columns // wide,),
            in_specs=[
                pl.BlockSpec((rows, channels), row(0)),
                pl.BlockSpec((rows, channels), row(1)),
                pl.BlockSpec((rows, channels), row(0)),
                pl.BlockSpec((rows, channels), row(1)),
                pl.BlockSpec((rows, N), row(0)),
                pl.BlockSpec((rows, N), row(1)),
                pl.BlockSpec(incoming.shape, lambda j, order: (0, 0, 0)),
                pl.BlockSpec((1, channels), lambda j, order: (0, 0)),
                pl.BlockSpec(memory_space=pl.ANY)
                if far
                else pl.BlockSpec((channels, wide), lambda j, order: (0, j)),
            ],
            out_specs=[
                pl.BlockSpec((rows, wide), lambda j, order: (0, j)),
                pl.BlockSpec((rows, wide), lambda j, order: (0, j)),
            ]
            + ([pl.BlockSpec((2 * rows, channels), lambda j, order: (0, 0))] if far else []),
            scratch_shapes=[pltpu.VMEM((channels, wide), BF), pltpu.SemaphoreType.DMA]
            if far
            else [normed],
        ),
        out_shape=[
            jax.ShapeDtypeStruct((rows, columns), BF),
            jax.ShapeDtypeStruct((rows, columns), F32),
        ]
        + ([jax.ShapeDtypeStruct((2 * rows, channels), BF)] if far else []),
        compiler_params=pltpu.CompilerParams(vmem_limit_bytes=WHOLE_VMEM),
        cost_estimate=pl.CostEstimate(
            flops=2 * 2 * rows * channels * columns,
            bytes_accessed=2 * channels * columns,
            transcendentals=0,
        ),
        name="finish_far" if far else "finish_near",
    )(order, own, own, lead, lead, c, c, incoming, gain, w)


def more_kernel(normed, w, theirs, mine):
    rows = theirs.shape[0]
    out = dot(normed[...], w[...])
    theirs[...] = out[:rows].astype(BF)
    mine[...] = out[rows:]


def project_more(normed, w, start, columns):
    rows2, channels = normed.shape
    rows = rows2 // 2
    wide = 512
    return pl.pallas_call(
        more_kernel,
        grid=(columns // wide,),
        in_specs=[
            pl.BlockSpec((rows2, channels), lambda j: (0, 0)),
            pl.BlockSpec((channels, wide), lambda j: (0, j + start // wide)),
        ],
        out_specs=[pl.BlockSpec((rows, wide), lambda j: (0, j))] * 2,
        out_shape=[
            jax.ShapeDtypeStruct((rows, columns), BF),
            jax.ShapeDtypeStruct((rows, columns), F32),
        ],
        compiler_params=pltpu.CompilerParams(vmem_limit_bytes=WHOLE_VMEM),
        cost_estimate=pl.CostEstimate(
            flops=2 * rows2 * channels * columns,
            bytes_accessed=2 * channels * columns,
            transcendentals=0,
        ),
        name="project_more",
    )(normed, w)


def early_kernel(kept, first, second, out):
    j = pl.program_id(0)

    @pl.when(j == 0)
    def _():
        out[...] = (kept[...] + first[...].astype(F32)).astype(BF)

    @pl.when(j == 1)
    def _():
        out[...] = (kept[...] + second[...].astype(F32)).astype(BF)


def early_sums(kept, first, second):
    rows, wide = first.shape
    return pl.pallas_call(
        early_kernel,
        grid=(2,),
        in_specs=[
            pl.BlockSpec((rows, wide), lambda j: (0, j)),
            pl.BlockSpec((rows, wide), lambda j: (0, 0)),
            pl.BlockSpec((rows, wide), lambda j: (0, 0)),
        ],
        out_specs=pl.BlockSpec((rows, wide), lambda j: (0, j)),
        out_shape=jax.ShapeDtypeStruct(kept.shape, BF),
        compiler_params=pltpu.CompilerParams(vmem_limit_bytes=VMEM_LIMIT),
        name="early_sums",
    )(kept, first, second)


def last_kernel(kept, third, filled, out):
    out[...] = (kept[...] + third[...].astype(F32)).astype(BF)


def last_sums(kept, third, filled):
    rows, wide = third.shape
    return pl.pallas_call(
        last_kernel,
        grid=(1,),
        in_specs=[
            pl.BlockSpec((rows, wide), lambda j: (0, 1)),
            pl.BlockSpec((rows, wide), lambda j: (0, 0)),
            pl.BlockSpec(memory_space=pl.ANY),
        ],
        out_specs=pl.BlockSpec((rows, wide), lambda j: (0, 1)),
        out_shape=jax.ShapeDtypeStruct(kept.shape, BF),
        input_output_aliases={2: 0},
        compiler_params=pltpu.CompilerParams(vmem_limit_bytes=VMEM_LIMIT),
        name="last_sums",
    )(kept, third, filled)


def incoming_states(msg, count):
    if count == msg.shape[0]:
        arrived = lax.all_to_all(msg, "seq", 0, 0, tiled=True)
        return lax.all_to_all(prefix(arrived), "seq", 0, 0, tiled=True)
    everyone = lax.all_gather(msg, "seq")
    mine = lax.axis_index("seq")

    def turn(j, total):
        part = everyone[j].astype(F32)
        decay = part[:, N:N + 1] + part[:, N + 8:N + 9]
        return jnp.where(j < mine, total * decay + part[:, :N], total)

    zero = jnp.zeros((msg.shape[0], N, LANES), F32)
    return lax.fori_loop(0, count - 1, turn, zero).astype(BF)


def per_device(
    seq_count,
    ssm_input,
    gate_input,
    step_raw,
    decay_log,
    state_in,
    state_out,
    skip_gain,
    norm_gain,
    out_weight,
):
    tok = ssm_input.shape[0]
    heads = decay_log.shape[0]
    b = state_in.reshape(tok, N)
    c = state_out.reshape(tok, N)
    msg, aux = local_states(step_raw.T, decay_log.reshape(1, heads), ssm_input, b)
    incoming = incoming_states(msg, seq_count)
    skip = jnp.repeat(skip_gain, P_SIZE).reshape(1, -1)
    own, lead = within(aux, ssm_input, b, c, gate_input, skip)

    me = lax.axis_index("head")
    order = jnp.stack([me ^ 3, me ^ 2, me ^ 1, me]).astype(jnp.int32)
    near = [(h, h ^ 1) for h in range(4)]
    far = [(h, h ^ 2) for h in range(4)]
    gain = norm_gain.reshape(1, -1)

    def paired(theirs, mine):
        return mine + lax.ppermute(theirs, "head", near).astype(F32)

    theirs, mine, normed = finish_project(
        order, True, own, lead, c, incoming, gain, out_weight, PIECES[0][1]
    )
    sent = [paired(theirs, mine).astype(BF)]
    sent.append(paired(*project_more(normed, out_weight, *PIECES[1])).astype(BF))
    normed, sent[0] = lax.optimization_barrier((normed, sent[0]))
    sent.append(paired(*project_more(normed, out_weight, *PIECES[2])).astype(BF))
    arrived = [lax.ppermute(part, "head", far) for part in sent[:2]]
    order, sent[2] = lax.optimization_barrier((order, sent[2]))
    arrived.append(lax.ppermute(sent[2], "head", far))
    kept = paired(
        *finish_project(
            order, False, own, lead, c, incoming, gain, out_weight, out_weight.shape[1]
        )
    )
    return last_sums(kept, arrived[2], early_sums(kept, arrived[0], arrived[1]))


def solution(mesh):
    in_specs = (
        P("seq", "head"),
        P("seq", "head"),
        P("seq", "head"),
        P("head"),
        P("seq", "head", None),
        P("seq", "head", None),
        P("head"),
        P("head"),
        P("head", None),
    )
    out_specs = P(("seq", "head"), None)
    return jax.shard_map(
        functools.partial(per_device, mesh.shape["seq"]),
        mesh=mesh,
        in_specs=in_specs,
        out_specs=out_specs,
        check_vma=False,
    )
```

profile of v0, /device:TPU:0, one launch (start us, length us, event | category | flops | bytes accessed | tf_op | source)
XLA Modules:
  0.0 94.1 jit_solution(9551382026890720084)
XLA Ops:
  0.0 4.9 %local_states.1 = (bf16[8,144,128]{2,1,0:T(8,128)(2,1)}, f32[48,512]{1,0:T(8,128)}) custom-call(f32[16,512]{1,0:T(8,128)} %bitcast.16, f32[1,16]{1,0:T(1,128)} %bitcast.19, f32[512,1024]{1,0:T(8,128)} %x_ref.3, f32[512,128]{1,0:T(8,128)} %bitcast.14), custom_call_target="tpu_custom_call" | custom-call | flops 400000000 | bytes 2800000 | tf_op jit(solution)/shard_map/local_states/pallas_call | solution.py:104
  4.9 17.6 %all_to_all.10.msg_ref = bf16[8,144,128]{2,1,0:T(8,128)(2,1)S(1)} all-to-all(bf16[8,144,128]{2,1,0:T(8,128)(2,1)} %get-tuple-element.25), channel_id=1, replica_groups=mesh['seq'=8,'head'=4] {'seq'}, dimensions={0} | all-to-all | bytes 589824 | tf_op jit(solution)/shard_map/all_to_all | solution.py:422
  23.3 3.4 %all-to-all-start.1 = ((bf16[8,128,128]{2,1,0:T(8,128)(2,1)}), bf16[8,128,128]{2,1,0:T(8,128)(2,1)S(1)}, u32[]{:S(2)}, u32[]{:S(2)}) async-start(bf16[8,128,128]{2,1,0:T(8,128)(2,1)} %prefix.1), calls=%async_computation.1 | async-start | bytes 524288 | tf_op jit(solution)/shard_map/all_to_all | solution.py:423
  27.5 1.2 %copy-done.5 = bf16[512,1024]{1,0:T(8,128)(2,1)S(1)} copy-done((bf16[512,1024]{1,0:T(8,128)(2,1)S(1)}, bf16[512,1024]{1,0:T(8,128)(2,1)}, u32[]{:S(2)}) %copy-start.5) | copy-done | bytes 1048600
  28.7 0.9 copy-done.6
  29.6 5.8 %within.1 = (f32[512,1024]{1,0:T(8,128)S(1)}, f32[512,1024]{1,0:T(8,128)S(1)}) custom-call(f32[48,512]{1,0:T(8,128)S(1)} %copy-done.6, f32[512,1024]{1,0:T(8,128)S(1)} %copy-done.3, f32[512,128]{1,0:T(8,128)S(1)} %bitcast.15, f32[512,128]{1,0:T(8,128)S(1)} %bitcast.13, bf16[512,1024]{1,0:T(8,128)(2,1)S(1)} %copy-done.5, f32[1,1024]{1,0:T(1,128)S(1)} %reshape_reshape.3.skip_ref), custom_call_target="tpu_custom_call" | custom-call | flops 2000000000 | bytes 5000000 | tf_op jit(solution)/shard_map/within/pallas_call | solution.py:221
  35.4 1.3 %copy-done = f32[512,1024]{1,0:T(8,128)} copy-done((f32[512,1024]{1,0:T(8,128)}, f32[512,1024]{1,0:T(8,128)S(1)}, u32[]{:S(2)}) %copy-start) | copy-done | bytes 2097176
  36.7 1.3 %copy-done.1 = f32[512,1024]{1,0:T(8,128)} copy-done((f32[512,1024]{1,0:T(8,128)}, f32[512,1024]{1,0:T(8,128)S(1)}, u32[]{:S(2)}) %copy-start.1) | copy-done | bytes 2097176
  38.8 5.6 %finish_far.1 = (bf16[128,1024]{1,0:T(8,128)(2,1)}, f32[128,1024]{1,0:T(8,128)}, bf16[256,1024]{1,0:T(8,128)(2,1)}) custom-call(s32[4]{0:T(128)} %pad_add_fusion.order, f32[512,1024]{1,0:T(8,128)} %copy-done, f32[512,1024]{1,0:T(8,128)} %copy-done, f32[512,1024]{1,0:T(8,128)} %copy-done.1, f32[512,1024]{1,0:T(8,128)} %copy-done.1, f32[512,128]{1,0:T(8,128)} %bitcast.9, ...), custom_call_target="tpu_custom_call" | custom-call | flops 536870912 | bytes 2097152 | tf_op jit(solution)/shard_map/finish_far/pallas_call | solution.py:294
  44.5 1.7 %collective-permute-done = bf16[128,1024]{1,0:T(8,128)(2,1)S(1)} collective-permute-done((bf16[128,1024]{1,0:T(8,128)(2,1)}, bf16[128,1024]{1,0:T(8,128)(2,1)S(1)}, u32[]{:S(2)}, u32[]{:S(2)}) %collective-permute-start) | collective-permute-done | bytes 262176 | tf_op jit(solution)/shard_map/ppermute | solution.py:464
  46.2 1.1 %add_convert_fusion.2 = bf16[128,1024]{1,0:T(8,128)(2,1)S(1)} fusion(f32[128,1024]{1,0:T(8,128)} %get-tuple-element.27, bf16[128,1024]{1,0:T(8,128)(2,1)S(1)} %collective-permute-done), kind=kLoop, calls=%fused_computation.3 | loop fusion | flops 393216 | bytes 1048576 | tf_op jit(solution)/shard_map/convert_element_type | solution.py:469
  47.3 5.0 %project_more.2 = (bf16[128,2048]{1,0:T(8,128)(2,1)}, f32[128,2048]{1,0:T(8,128)}) custom-call(bf16[256,1024]{1,0:T(8,128)(2,1)} %get-tuple-element.29.normed, bf16[1024,4096]{1,0:T(8,128)(2,1)} %w.7), custom_call_target="tpu_custom_call" | custom-call | flops 1073741824 | bytes 4194304 | tf_op jit(solution)/shard_map/project_more/pallas_call | solution.py:347
  52.5 2.0 %collective-permute-done.1 = bf16[128,2048]{1,0:T(8,128)(2,1)S(1)} collective-permute-done((bf16[128,2048]{1,0:T(8,128)(2,1)}, bf16[128,2048]{1,0:T(8,128)(2,1)S(1)}, u32[]{:S(2)}, u32[]{:S(2)}) %collective-permute-start.1) | collective-permute-done | bytes 524320 | tf_op jit(solution)/shard_map/ppermute | solution.py:464
  54.4 1.3 %add_convert_fusion = bf16[128,2048]{1,0:T(8,128)(2,1)S(1)} fusion(f32[128,2048]{1,0:T(8,128)} %get-tuple-element.30, bf16[128,2048]{1,0:T(8,128)(2,1)S(1)} %collective-permute-done.1), kind=kLoop, calls=%fused_computation.1 | loop fusion | flops 786432 | bytes 2097152 | tf_op jit(solution)/shard_map/convert_element_type | solution.py:472
  55.8 8.6 %finish_near.1 = (bf16[128,4096]{1,0:T(8,128)(2,1)}, f32[128,4096]{1,0:T(8,128)}) custom-call(s32[4]{0:T(128)} %pad_add_fusion.order, f32[512,1024]{1,0:T(8,128)} %copy-done, f32[512,1024]{1,0:T(8,128)} %copy-done, f32[512,1024]{1,0:T(8,128)} %copy-done.1, f32[512,1024]{1,0:T(8,128)} %copy-done.1, f32[512,128]{1,0:T(8,128)} %bitcast.11, ...), custom_call_target="tpu_custom_call" | custom-call | flops 2147483648 | bytes 8388608 | tf_op jit(solution)/shard_map/finish_near/pallas_call | solution.py:294
  64.5 3.2 %project_more.3 = (bf16[128,1024]{1,0:T(8,128)(2,1)}, f32[128,1024]{1,0:T(8,128)}) custom-call(bf16[256,1024]{1,0:T(8,128)(2,1)} %get-tuple-element.29.normed, bf16[1024,4096]{1,0:T(8,128)(2,1)} %w.7), custom_call_target="tpu_custom_call" | custom-call | flops 536870912 | bytes 2097152 | tf_op jit(solution)/shard_map/project_more/pallas_call | solution.py:347
  68.1 1.5 %collective-permute-start.4 = (bf16[128,1024]{1,0:T(8,128)(2,1)S(1)}, bf16[128,1024]{1,0:T(8,128)(2,1)S(1)}, u32[]{:S(2)}, u32[]{:S(2)}) collective-permute-start(bf16[128,1024]{1,0:T(8,128)(2,1)S(1)} %add_convert_fusion.2), channel_id=1, source_target_pairs={{0,2},{1,3},{2,0},{3,1},{4,6},{5,7},{6,4},{7,5},{8,10},{9,11},{10,... | collective-permute-start | bytes 786440 | tf_op jit(solution)/shard_map/ppermute | solution.py:473
  69.6 1.1 %add_convert_fusion.1 = bf16[128,1024]{1,0:T(8,128)(2,1)S(1)} fusion(f32[128,1024]{1,0:T(8,128)} %get-tuple-element.37, bf16[128,1024]{1,0:T(8,128)(2,1)S(1)} %collective-permute-done.5), kind=kLoop, calls=%fused_computation.2 | loop fusion | flops 393216 | bytes 1048576 | tf_op jit(solution)/shard_map/convert_element_type | solution.py:470
  70.7 1.4 %collective-permute-start.6 = (bf16[128,1024]{1,0:T(8,128)(2,1)S(1)}, bf16[128,1024]{1,0:T(8,128)(2,1)S(1)}, u32[]{:S(2)}, u32[]{:S(2)}) collective-permute-start(bf16[128,1024]{1,0:T(8,128)(2,1)S(1)} %add_convert_fusion.1), channel_id=1, source_target_pairs={{0,2},{1,3},{2,0},{3,1},{4,6},{5,7},{6,4},{7,5},{8,10},{9,11},{10,... | collective-permute-start | bytes 786440 | tf_op jit(solution)/shard_map/ppermute | solution.py:473
  73.0 4.2 %collective-permute-done.4.first = bf16[128,1024]{1,0:T(8,128)(2,1)S(1)} collective-permute-done((bf16[128,1024]{1,0:T(8,128)(2,1)S(1)}, bf16[128,1024]{1,0:T(8,128)(2,1)S(1)}, u32[]{:S(2)}, u32[]{:S(2)}) %collective-permute-start.4) | collective-permute-done | bytes 262176 | tf_op jit(solution)/shard_map/ppermute | solution.py:473
  77.2 5.6 %collective-permute-done.6.second = bf16[128,1024]{1,0:T(8,128)(2,1)S(1)} collective-permute-done((bf16[128,1024]{1,0:T(8,128)(2,1)S(1)}, bf16[128,1024]{1,0:T(8,128)(2,1)S(1)}, u32[]{:S(2)}, u32[]{:S(2)}) %collective-permute-start.6) | collective-permute-done | bytes 262176 | tf_op jit(solution)/shard_map/ppermute | solution.py:473
  82.8 0.9 early_sums.1.filled
  83.8 9.5 %collective-permute-done.3.third = bf16[128,2048]{1,0:T(8,128)(2,1)S(1)} collective-permute-done((bf16[128,2048]{1,0:T(8,128)(2,1)S(1)}, bf16[128,2048]{1,0:T(8,128)(2,1)S(1)}, u32[]{:S(2)}, u32[]{:S(2)}) %collective-permute-start.3) | collective-permute-done | bytes 524320 | tf_op jit(solution)/shard_map/ppermute | solution.py:475
  93.3 0.9 last_sums.1
  (29 shorter events, 3.8 us)
Async XLA Ops:
  0.0 27.5 %copy-start.3 = (f32[512,1024]{1,0:T(8,128)S(1)}, f32[512,1024]{1,0:T(8,128)}, u32[]{:S(2)}) copy-start(f32[512,1024]{1,0:T(8,128)} %x_ref.3) | copy-start | bytes 6291460
  0.0 27.5 %copy-start.4 = (f32[512,1,128]{2,1,0:T(1,128)S(1)}, f32[512,1,128]{2,1,0:T(1,128)}, u32[]{:S(2)}) copy-start(f32[512,1,128]{2,1,0:T(1,128)} %param.13) | copy-start | bytes 786436
  0.0 26.7 %copy-start.9 = (f32[16]{0:T(128)S(1)}, f32[16]{0:T(128)}, u32[]{:S(2)}) copy-start(f32[16]{0:T(128)} %param.15) | copy-start | bytes 196
  0.0 27.5 %copy-start.2 = (f32[512,1,128]{2,1,0:T(1,128)S(1)}, f32[512,1,128]{2,1,0:T(1,128)}, u32[]{:S(2)}) copy-start(f32[512,1,128]{2,1,0:T(1,128)} %param.14) | copy-start | bytes 786436
  23.3 14.8 %all-to-all-start.1 = ((bf16[8,128,128]{2,1,0:T(8,128)(2,1)}), bf16[8,128,128]{2,1,0:T(8,128)(2,1)S(1)}, u32[]{:S(2)}, u32[]{:S(2)}) async-start(bf16[8,128,128]{2,1,0:T(8,128)(2,1)} %prefix.1), calls=%async_computation.1 | async-start | bytes 524288 | tf_op jit(solution)/shard_map/all_to_all | solution.py:423
  27.5 1.2 %copy-start.5 = (bf16[512,1024]{1,0:T(8,128)(2,1)S(1)}, bf16[512,1024]{1,0:T(8,128)(2,1)}, u32[]{:S(2)}) copy-start(bf16[512,1024]{1,0:T(8,128)(2,1)} %gate_ref.1) | copy-start | bytes 3145732
  28.7 0.9 copy-start.6
  35.4 1.3 %copy-start = (f32[512,1024]{1,0:T(8,128)}, f32[512,1024]{1,0:T(8,128)S(1)}, u32[]{:S(2)}) copy-start(f32[512,1024]{1,0:T(8,128)S(1)} %get-tuple-element.23.o0.o1) | copy-start | bytes 6291460
  36.7 1.3 %copy-start.1 = (f32[512,1024]{1,0:T(8,128)}, f32[512,1024]{1,0:T(8,128)S(1)}, u32[]{:S(2)}) copy-start(f32[512,1024]{1,0:T(8,128)S(1)} %get-tuple-element.24.l0.l1) | copy-start | bytes 6291460
  38.0 0.7 copy-start.7
  44.4 1.8 %collective-permute-start = (bf16[128,1024]{1,0:T(8,128)(2,1)}, bf16[128,1024]{1,0:T(8,128)(2,1)S(1)}, u32[]{:S(2)}, u32[]{:S(2)}) collective-permute-start(bf16[128,1024]{1,0:T(8,128)(2,1)} %get-tuple-element.28), channel_id=1, source_target_pairs={{0,1},{1,0},{2,3},{3,2},{4,5},{5,4},{6,7},{7,6},{8,9},{9,8},{10,11... | collective-permute-start | bytes 786440 | tf_op jit(solution)/shard_map/ppermute | solution.py:464
  52.3 2.1 %collective-permute-start.1 = (bf16[128,2048]{1,0:T(8,128)(2,1)}, bf16[128,2048]{1,0:T(8,128)(2,1)S(1)}, u32[]{:S(2)}, u32[]{:S(2)}) collective-permute-start(bf16[128,2048]{1,0:T(8,128)(2,1)} %get-tuple-element.31), channel_id=1, source_target_pairs={{0,1},{1,0},{2,3},{3,2},{4,5},{5,4},{6,7},{7,6},{8,9},{9,8},{10,11... | collective-permute-start | bytes 1572872 | tf_op jit(solution)/shard_map/ppermute | solution.py:464
  64.4 8.4 %collective-permute-start.2 = (bf16[128,4096]{1,0:T(8,128)(2,1)}, bf16[128,4096]{1,0:T(8,128)(2,1)S(1)}, u32[]{:S(2)}, u32[]{:S(2)}) collective-permute-start(bf16[128,4096]{1,0:T(8,128)(2,1)} %get-tuple-element.34), channel_id=1, source_target_pairs={{0,1},{1,0},{2,3},{3,2},{4,5},{5,4},{6,7},{7,6},{8,9},{9,8},{10,11... | collective-permute-start | bytes 3145736 | tf_op jit(solution)/shard_map/ppermute | solution.py:464
  64.5 8.3 %copy-start.8 = (f32[128,4096]{1,0:T(8,128)S(1)}, f32[128,4096]{1,0:T(8,128)}, u32[]{:S(2)}) copy-start(f32[128,4096]{1,0:T(8,128)} %get-tuple-element.33) | copy-start | bytes 6291460
  67.7 1.9 %collective-permute-start.5 = (bf16[128,1024]{1,0:T(8,128)(2,1)}, bf16[128,1024]{1,0:T(8,128)(2,1)S(1)}, u32[]{:S(2)}, u32[]{:S(2)}) collective-permute-start(bf16[128,1024]{1,0:T(8,128)(2,1)} %get-tuple-element.38), channel_id=1, source_target_pairs={{0,1},{1,0},{2,3},{3,2},{4,5},{5,4},{6,7},{7,6},{8,9},{9,8},{10,11... | collective-permute-start | bytes 786440 | tf_op jit(solution)/shard_map/ppermute | solution.py:464
  68.1 9.2 %collective-permute-start.4 = (bf16[128,1024]{1,0:T(8,128)(2,1)S(1)}, bf16[128,1024]{1,0:T(8,128)(2,1)S(1)}, u32[]{:S(2)}, u32[]{:S(2)}) collective-permute-start(bf16[128,1024]{1,0:T(8,128)(2,1)S(1)} %add_convert_fusion.2), channel_id=1, source_target_pairs={{0,2},{1,3},{2,0},{3,1},{4,6},{5,7},{6,4},{7,5},{8,10},{9,11},{10,... | collective-permute-start | bytes 786440 | tf_op jit(solution)/shard_map/ppermute | solution.py:473
  70.7 12.1 %collective-permute-start.6 = (bf16[128,1024]{1,0:T(8,128)(2,1)S(1)}, bf16[128,1024]{1,0:T(8,128)(2,1)S(1)}, u32[]{:S(2)}, u32[]{:S(2)}) collective-permute-start(bf16[128,1024]{1,0:T(8,128)(2,1)S(1)} %add_convert_fusion.1), channel_id=1, source_target_pairs={{0,2},{1,3},{2,0},{3,1},{4,6},{5,7},{6,4},{7,5},{8,10},{9,11},{10,... | collective-permute-start | bytes 786440 | tf_op jit(solution)/shard_map/ppermute | solution.py:473
  72.1 21.1 %collective-permute-start.3 = (bf16[128,2048]{1,0:T(8,128)(2,1)S(1)}, bf16[128,2048]{1,0:T(8,128)(2,1)S(1)}, u32[]{:S(2)}, u32[]{:S(2)}) collective-permute-start(bf16[128,2048]{1,0:T(8,128)(2,1)S(1)} %add_convert_fusion), channel_id=1, source_target_pairs={{0,2},{1,3},{2,0},{3,1},{4,6},{5,7},{6,4},{7,5},{8,10},{9,11},{10,... | collective-permute-start | bytes 1572872 | tf_op jit(solution)/shard_map/ppermute | solution.py:475
where the time goes:
time: 94.9 us; the launch traced here: 94.1 us
  Pallas kernels  35.7 us (38%)
  waiting for transfers between devices  23 us (24%)
  blocking collectives  17.6 us (19%)
  starting transfers between devices  7.74 us (8%)
  local copies, waits for them, and re-layouts  5.65 us (6%)
  other arithmetic  4.34 us (5%)
    all_to_all x1, blocking collectives, incoming_states(): arrived = lax.all_to_all(msg, 'seq', 0, 0, tiled=True)  17.6 us
    pallas_call x2, Pallas kernels, finish_project(): pl.pallas_call(far_kernel if far else near_kernel, grid_spec=pltpu.Prefet...  14.2 us
    ppermute x2, waiting for transfers between devices, per_device(): arrived = [lax.ppermute(part, 'head', far) for part in sent[:2]]  9.81 us
    ppermute x1, waiting for transfers between devices, per_device(): arrived.append(lax.ppermute(sent[2], 'head', far))  9.5 us
    pallas_call x2, Pallas kernels, project_more(): pl.pallas_call(more_kernel, grid=(columns // wide,), in_specs=[pl.BlockSp...  8.14 us
    pallas_call x1, Pallas kernels, within(): pl.pallas_call(within_kernel, grid=(channels // width,), in_specs=[pl.Blo...  5.81 us
    unnamed x20, local copies, waits for them, and re-layouts  5.5 us
    pallas_call x1, Pallas kernels, local_states(): pl.pallas_call(state_kernel, grid=(x.shape[1] // width,), in_specs=[pl.Bl...  4.91 us
  transfers between devices with their start and end apart: 8, of which 5 were waited for; matrix products, arithmetic and copies ran while one was open for 2% of the time, Pallas kernels for 11%

commit v1 on v0

v1 whole, which is shorter than its diff:
```python
import functools

import jax
import jax.numpy as jnp
from jax import lax
from jax.experimental import pallas as pl
from jax.experimental.pallas import tpu as pltpu
from jax.sharding import PartitionSpec as P

P_SIZE = 64
N = 128
CHUNK = 128
LANES = 128
BF = jnp.bfloat16
F32 = jnp.float32
VMEM_LIMIT = 24 * 1024 * 1024
WHOLE_VMEM = 60 * 1024 * 1024
PIECES = ((0, 1024), (1024, 1024), (2048, 2048))


def dot(a, b, contract=((1,), (0,)), precision=None):
    return lax.dot_general(a, b, (contract, ((), ())), precision=precision, preferred_element_type=F32)


def split2(v):
    hi = v.astype(BF)
    return hi, (v - hi.astype(F32)).astype(BF)


def split3(v):
    hi, rest = v.astype(BF), v
    rest = v - hi.astype(F32)
    mid = rest.astype(BF)
    return hi, mid, (rest - mid.astype(F32)).astype(BF)


def pick(rows, lanes, heads, per_head, first):
    r = lax.broadcasted_iota(jnp.int32, (rows, lanes), 0) % heads
    l = lax.broadcasted_iota(jnp.int32, (rows, lanes), 1) // per_head + first
    return jnp.where(r == l, 1.0, 0.0).astype(BF)


def step_vectors(raw, rate_row, wk, aux_ref):
    heads, tok = raw.shape
    chunks = tok // CHUNK
    step = jnp.maximum(raw, 0.0) + jnp.log1p(jnp.exp(-jnp.abs(raw)))
    r = lax.broadcasted_iota(jnp.int32, (heads, heads), 0)
    l = lax.broadcasted_iota(jnp.int32, (heads, heads), 1)
    rate = jnp.sum(jnp.where(r == l, rate_row, 0.0), axis=1, keepdims=True)
    logs = -step * jnp.exp(rate)
    parts = split3(logs)
    stacked = jnp.concatenate(
        [p[:, c * CHUNK:(c + 1) * CHUNK] for c in range(chunks) for p in parts], axis=0
    )
    s = lax.broadcasted_iota(jnp.int32, (CHUNK, 2 * CHUNK), 0)
    t = lax.broadcasted_iota(jnp.int32, (CHUNK, 2 * CHUNK), 1)
    tri = jnp.where(jnp.where(t < CHUNK, t - s, s - t + (CHUNK - 1)) >= 0, 1.0, 0.0).astype(BF)
    sums = dot(stacked, tri)
    pre, suf = [], []
    for c in range(chunks):
        base = 3 * heads * c
        total = (
            sums[base:base + heads] + sums[base + heads:base + 2 * heads]
        ) + sums[base + 2 * heads:base + 3 * heads]
        pre.append(total[:, :CHUNK])
        suf.append(total[:, CHUNK:])
    after = jnp.zeros((heads, 1), F32)
    for c in reversed(range(chunks)):
        w = step[:, c * CHUNK:(c + 1) * CHUNK] * jnp.exp(suf[c] + after)
        hi, lo = split2(w)
        wk[:heads, c * CHUNK:(c + 1) * CHUNK] = hi
        wk[heads:, c * CHUNK:(c + 1) * CHUNK] = lo
        after = after + pre[c][:, CHUNK - 1:]
    hi, lo = split2(jnp.broadcast_to(jnp.exp(after), (heads, CHUNK)))
    wk[:heads, tok:] = hi
    wk[heads:, tok:] = lo
    aux_ref[:heads] = step
    aux_ref[heads:2 * heads] = jnp.concatenate(pre, axis=1)
    aux_ref[2 * heads:] = jnp.concatenate(suf, axis=1)


def tail_rows(decays):
    r = lax.broadcasted_iota(jnp.int32, (16, LANES), 0)
    tail = jnp.zeros((16, LANES), F32)
    for k, decay in enumerate(decays):
        hi, lo = split2(decay)
        tail = jnp.where(r == 2 * k, hi.astype(F32), tail)
        tail = jnp.where(r == 2 * k + 1, lo.astype(F32), tail)
    return tail.astype(BF)


def decays_of(msg):
    blocks = (msg.shape[0] - 16) // N
    tail = msg[blocks * N:].astype(F32)
    return [tail[2 * k:2 * k + 1] + tail[2 * k + 1:2 * k + 2] for k in range(blocks)]


def half_message(x_ref, b, wk, first_head, msg):
    tok, lanes = x_ref.shape
    heads2 = wk.shape[0]
    width = 256
    decays = []
    for g in range(lanes // width):
        chosen = pick(heads2, width, heads2 // 2, P_SIZE, first_head + g * (width // P_SIZE))
        spread = dot(wk[...], chosen, ((0,), (0,)))
        weighted = (x_ref[:, g * width:(g + 1) * width] * spread[:tok]).astype(BF)
        state = dot(b, weighted, ((0,), (0,)))
        for i in range(width // LANES):
            k = g * (width // LANES) + i
            msg[k * N:(k + 1) * N] = state[:, i * LANES:(i + 1) * LANES].astype(BF)
            decays.append(spread[tok:tok + 1, i * LANES:(i + 1) * LANES])
    msg[msg.shape[0] - 16:] = tail_rows(decays)


def half_kernel(give, raw, rate, x, b, msg, wk, aux, raw_v, rate_v, x_v, b_v, sems):
    lanes = x_v.shape[1]
    mine = lax.axis_index("seq") % 2
    half = 1 - mine if give else mine
    loads = [
        pltpu.make_async_copy(b, b_v, sems.at[0]),
        pltpu.make_async_copy(
            x.at[:, pl.ds(pl.multiple_of(half * lanes, lanes), lanes)], x_v, sems.at[1]
        ),
    ]
    if give:
        loads += [
            pltpu.make_async_copy(raw, raw_v, sems.at[2]),
            pltpu.make_async_copy(rate, rate_v, sems.at[3]),
        ]
    for load in reversed(loads):
        load.start()
    if give:
        loads[2].wait()
        loads[3].wait()
        step_vectors(raw_v[...], rate_v[...], wk, aux)
    loads[0].wait()
    loads[1].wait()
    half_message(x_v, b_v[...].astype(BF), wk, half * (lanes // P_SIZE), msg)


def give_kernel(raw, rate, x, b, msg, wk, aux, raw_v, rate_v, x_v, b_v, sems):
    half_kernel(True, raw, rate, x, b, msg, wk, aux, raw_v, rate_v, x_v, b_v, sems)


def keep_kernel(wk, x, b, msg, x_v, b_v, sems):
    half_kernel(False, None, None, x, b, msg, wk, None, None, None, x_v, b_v, sems)


HBM = pl.BlockSpec(memory_space=pltpu.HBM)


def give_states(raw, rate, x, b):
    heads, tok = raw.shape
    lanes = x.shape[1] // 2
    return pl.pallas_call(
        give_kernel,
        in_specs=[HBM] * 4,
        out_shape=[
            jax.ShapeDtypeStruct((lanes + 16, LANES), BF),
            jax.ShapeDtypeStruct((2 * heads, tok + CHUNK), BF),
            jax.ShapeDtypeStruct((3 * heads, tok), F32),
        ],
        scratch_shapes=[
            pltpu.VMEM((heads, tok), F32),
            pltpu.VMEM((1, heads), F32),
            pltpu.VMEM((tok, lanes), F32),
            pltpu.VMEM((tok, N), F32),
            pltpu.SemaphoreType.DMA((4,)),
        ],
        compiler_params=pltpu.CompilerParams(vmem_limit_bytes=WHOLE_VMEM),
        cost_estimate=pl.CostEstimate(flops=200_000_000, bytes_accessed=1_500_000, transcendentals=0),
        name="give_states",
    )(raw, rate, x, b)


def keep_states(wk, x, b):
    tok = x.shape[0]
    lanes = x.shape[1] // 2
    return pl.pallas_call(
        keep_kernel,
        in_specs=[pl.BlockSpec(memory_space=pltpu.VMEM), HBM, HBM],
        out_shape=jax.ShapeDtypeStruct((lanes + 16, LANES), BF),
        scratch_shapes=[
            pltpu.VMEM((tok, lanes), F32),
            pltpu.VMEM((tok, N), F32),
            pltpu.SemaphoreType.DMA((2,)),
        ],
        compiler_params=pltpu.CompilerParams(vmem_limit_bytes=VMEM_LIMIT),
        cost_estimate=pl.CostEstimate(flops=200_000_000, bytes_accessed=1_500_000, transcendentals=0),
        name="keep_states",
    )(wk, x, b)


def link(later, earlier, out):
    ahead, behind = decays_of(later), decays_of(earlier)
    for k, decay in enumerate(ahead):
        rows = slice(k * N, (k + 1) * N)
        out[rows] = (later[rows].astype(F32) + decay * earlier[rows].astype(F32)).astype(BF)
    out[len(ahead) * N:] = tail_rows([p * q for p, q in zip(ahead, behind)])


def pair_kernel(own, come, out):
    odd = lax.axis_index("seq") % 2

    @pl.when(odd == 0)
    def _():
        link(come, own, out)

    @pl.when(odd == 1)
    def _():
        link(own, come, out)


def end_kernel(last, before, own, come, mine, theirs):
    blocks = mine.shape[0] // N
    odd = lax.axis_index("seq") % 2

    def fill(even_section, ahead_ref, behind_ref):
        step, span = decays_of(last), decays_of(even_section)
        for k in range(blocks):
            rows = slice(k * N, (k + 1) * N)
            start = last[rows].astype(F32)
            if before is not None:
                start = start + step[k] * before[rows].astype(F32)
            ahead_ref[rows] = start.astype(BF)
            behind_ref[rows] = (even_section[rows].astype(F32) + span[k] * start).astype(BF)

    @pl.when(odd == 0)
    def _():
        fill(own, mine, theirs)

    @pl.when(odd == 1)
    def _():
        fill(come, theirs, mine)


def scan_call(kernel, operands, shapes, name):
    return pl.pallas_call(
        kernel,
        out_shape=[jax.ShapeDtypeStruct(shape, BF) for shape in shapes],
        compiler_params=pltpu.CompilerParams(vmem_limit_bytes=VMEM_LIMIT),
        cost_estimate=pl.CostEstimate(flops=500_000, bytes_accessed=400_000, transcendentals=0),
        name=name,
    )(*operands)


def incoming_states(give, keep, count, hold):
    pair = [(s, s ^ 1) for s in range(count)]
    come = lax.ppermute(give, "seq", pair)
    run = scan_call(pair_kernel, (keep, come), [keep.shape], "join_pair")[0]
    start, distance = None, 2
    while distance < count:
        got = lax.ppermute(run, "seq", [(s, s + distance) for s in range(count - distance)])
        if distance * 2 >= count:
            break
        run = scan_call(link, (run, got), [keep.shape], "join_run")[0]
        start = got if start is None else scan_call(link, (start, got), [keep.shape], "join_start")[0]
        distance *= 2
    hold, got = hold(got)
    half = (keep.shape[0] - 16, LANES)
    mine, theirs = scan_call(end_kernel, (start, got, keep, come), [half, half], "join_end")
    return hold, mine, lax.ppermute(theirs, "seq", pair)


def within_kernel(aux_ref, x_ref, b_ref, c_ref, gate_ref, skip_ref, own_ref, lead_ref, scores, trip, duo, lines):
    g = pl.program_id(0)
    tok, width = x_ref.shape
    heads = aux_ref.shape[0] // 3
    chunks = tok // CHUNK
    here = width // P_SIZE

    @pl.when(g == 0)
    def _():
        before = jnp.zeros((heads, 1), F32)
        i = lax.broadcasted_iota(jnp.int32, (CHUNK, CHUNK), 0)
        j = lax.broadcasted_iota(jnp.int32, (CHUNK, CHUNK), 1)
        for c in range(chunks):
            cut = slice(c * CHUNK, (c + 1) * CHUNK)
            step, pre, suf = (aux_ref[k * heads:(k + 1) * heads, cut] for k in range(3))
            trip[c] = jnp.concatenate([v for v in split3(pre)], axis=0)
            for k, value in enumerate(
                (step, step * jnp.exp(suf), jnp.exp(pre), jnp.exp(pre + before))
            ):
                hi, lo = split2(value)
                duo[c, :heads, k * CHUNK:(k + 1) * CHUNK] = hi
                duo[c, heads:, k * CHUNK:(k + 1) * CHUNK] = lo
            before = before + pre[:, CHUNK - 1:]
            for k in range(heads // here):
                lines[k, :here, cut] = pre[k * here:(k + 1) * here]
            raw = dot(c_ref[cut], b_ref[cut], ((1,), (1,)), lax.Precision.HIGHEST)
            scores[c] = jnp.where(i >= j, raw, 0.0)

    spread = pick(2 * heads, width, heads, P_SIZE, g * here)
    columns = pick(3 * heads, here * CHUNK, heads, CHUNK, g * here)
    lane = lax.broadcasted_iota(jnp.int32, (CHUNK, LANES), 1)
    state = jnp.zeros((N, width), F32)
    mine = lines[g]
    for c in range(chunks):
        cut = slice(c * CHUNK, (c + 1) * CHUNK)
        wide = dot(duo[c], spread, ((0,), (0,)))
        x = x_ref[cut]
        stepped = x * wide[:CHUNK]
        lead = wide[2 * CHUNK:3 * CHUNK]
        tall = dot(trip[c], columns, ((0,), (0,)))
        outs = []
        for pair in range(here // 2):
            mixes = []
            for h in (2 * pair, 2 * pair + 1):
                gap = tall[:, h * CHUNK:(h + 1) * CHUNK] - mine[h:h + 1, cut]
                mixes.append((scores[c] * jnp.exp(jnp.minimum(gap, 0.0))).astype(BF))
            both = stepped[:, pair * LANES:(pair + 1) * LANES]
            stacked = jnp.concatenate(
                [
                    jnp.where(lane < P_SIZE, both, 0.0).astype(BF),
                    jnp.where(lane < P_SIZE, 0.0, both).astype(BF),
                ],
                axis=0,
            )
            outs.append(dot(jnp.concatenate(mixes, axis=1), stacked))
        y = jnp.concatenate(outs, axis=1) + skip_ref[...] * x
        if c:
            y = y + lead * dot(c_ref[cut].astype(BF), state.astype(BF))
        v = gate_ref[cut].astype(F32)
        silu = v / (1.0 + jnp.exp(-v))
        own_ref[cut] = y * silu
        lead_ref[cut] = wide[3 * CHUNK:] * silu
        if c < chunks - 1:
            weighted = (x * wide[CHUNK:2 * CHUNK]).astype(BF)
            added = dot(b_ref[cut].astype(BF), weighted, ((0,), (0,)))
            state = state * lead[CHUNK - 1:] + added


def within(aux, x, b, c, gate, skip):
    tok, channels = x.shape
    heads = aux.shape[0] // 3
    width = 256
    chunks = tok // CHUNK
    return pl.pallas_call(
        within_kernel,
        grid=(channels // width,),
        in_specs=[
            pl.BlockSpec((3 * heads, tok), lambda g: (0, 0)),
            pl.BlockSpec((tok, width), lambda g: (0, g)),
            pl.BlockSpec((tok, N), lambda g: (0, 0)),
            pl.BlockSpec((tok, N), lambda g: (0, 0)),
            pl.BlockSpec((tok, width), lambda g: (0, g)),
            pl.BlockSpec((1, width), lambda g: (0, g)),
        ],
        out_specs=[pl.BlockSpec((tok, width), lambda g: (0, g))] * 2,
        out_shape=[jax.ShapeDtypeStruct((tok, channels), F32)] * 2,
        scratch_shapes=[
            pltpu.VMEM((chunks, CHUNK, CHUNK), F32),
            pltpu.VMEM((chunks, 3 * heads, CHUNK), BF),
            pltpu.VMEM((chunks, 2 * heads, 4 * CHUNK), BF),
            pltpu.VMEM((channels // width, 8, tok), F32),
        ],
        compiler_params=pltpu.CompilerParams(vmem_limit_bytes=VMEM_LIMIT),
        cost_estimate=pl.CostEstimate(
            flops=2_000_000_000, bytes_accessed=5_000_000, transcendentals=1_000_000
        ),
        name="within",
    )(aux, x, b, c, gate, skip)


def finish_rows(own, lead, c, incoming, gain):
    c = c.astype(BF)
    blocks = incoming.shape[1] // N
    carried = jnp.concatenate(
        [dot(c, incoming[h, k * N:(k + 1) * N]) for h in range(2) for k in range(blocks)], axis=1
    )
    gated = own + lead * carried
    mean = jnp.mean(gated * gated, axis=1, keepdims=True)
    return (gated * lax.rsqrt(mean + 1e-05) * gain).astype(BF)


def start_weights(w, start, weights, sems):
    count, _, wide = weights.shape
    loads = [
        pltpu.make_async_copy(w.at[:, start + k * wide:start + (k + 1) * wide], weights.at[k], sems.at[k])
        for k in range(count)
    ]
    for load in loads:
        load.start()
    return loads


def project_rows(normed, loads, weights, theirs, mine):
    rows = theirs.shape[0]
    wide = weights.shape[2]
    for k, load in enumerate(loads):
        load.wait()
        out = dot(normed[...], weights[k])
        theirs[:, k * wide:(k + 1) * wide] = out[:rows].astype(BF)
        mine[:, k * wide:(k + 1) * wide] = out[rows:]


def finish_kernel(
    order, o0, o1, l0, l1, c0, c1, here, there, gain, w, theirs, mine, normed, incoming, weights, sems
):
    rows = o0.shape[0]
    loads = start_weights(w, 0, weights, sems)
    odd = lax.axis_index("seq") % 2
    incoming[odd] = here[...]
    incoming[1 - odd] = there[...]
    normed[:rows] = finish_rows(o0[...], l0[...], c0[...], incoming, gain[...])
    normed[rows:] = finish_rows(o1[...], l1[...], c1[...], incoming, gain[...])
    project_rows(normed, loads, weights, theirs, mine)


def finish_project(order, first, own, lead, c, here, there, gain, w, columns, name):
    channels = own.shape[1]
    rows = CHUNK
    wide = 512

    def row(k):
        return lambda j, order: (order[first + k], 0)

    def whole(j, order):
        return (0, 0)

    return pl.pallas_call(
        finish_kernel,
        grid_spec=pltpu.PrefetchScalarGridSpec(
            num_scalar_prefetch=1,
            grid=(1,),
            in_specs=[
                pl.BlockSpec((rows, channels), row(0)),
                pl.BlockSpec((rows, channels), row(1)),
                pl.BlockSpec((rows, channels), row(0)),
                pl.BlockSpec((rows, channels), row(1)),
                pl.BlockSpec((rows, N), row(0)),
                pl.BlockSpec((rows, N), row(1)),
                pl.BlockSpec(here.shape, whole),
                pl.BlockSpec(there.shape, whole),
                pl.BlockSpec((1, channels), whole),
                HBM,
            ],
            out_specs=[
                pl.BlockSpec((rows, columns), whole),
                pl.BlockSpec((rows, columns), whole),
                pl.BlockSpec((2 * rows, channels), whole),
            ],
            scratch_shapes=[
                pltpu.VMEM((2,) + here.shape, BF),
                pltpu.VMEM((columns // wide, channels, wide), BF),
                pltpu.SemaphoreType.DMA((columns // wide,)),
            ],
        ),
        out_shape=[
            jax.ShapeDtypeStruct((rows, columns), BF),
            jax.ShapeDtypeStruct((rows, columns), F32),
            jax.ShapeDtypeStruct((2 * rows, channels), BF),
        ],
        compiler_params=pltpu.CompilerParams(vmem_limit_bytes=VMEM_LIMIT),
        cost_estimate=pl.CostEstimate(
            flops=2 * 2 * rows * channels * columns,
            bytes_accessed=2 * channels * columns,
            transcendentals=0,
        ),
        name=name,
    )(order, own, own, lead, lead, c, c, here, there, gain, w)


def more_kernel(start, normed, w, theirs, mine, weights, sems):
    project_rows(normed, start_weights(w, start, weights, sems), weights, theirs, mine)


def project_more(normed, w, start, columns):
    rows2, channels = normed.shape
    rows = rows2 // 2
    wide = 512
    return pl.pallas_call(
        functools.partial(more_kernel, start),
        in_specs=[pl.BlockSpec(memory_space=pltpu.VMEM), HBM],
        out_shape=[
            jax.ShapeDtypeStruct((rows, columns), BF),
            jax.ShapeDtypeStruct((rows, columns), F32),
        ],
        scratch_shapes=[
            pltpu.VMEM((columns // wide, channels, wide), BF),
            pltpu.SemaphoreType.DMA((columns // wide,)),
        ],
        compiler_params=pltpu.CompilerParams(vmem_limit_bytes=VMEM_LIMIT),
        cost_estimate=pl.CostEstimate(
            flops=2 * rows2 * channels * columns,
            bytes_accessed=2 * channels * columns,
            transcendentals=0,
        ),
        name="project_more",
    )(normed, w)


def pass_kernel(*refs):
    pass


def await_piece(piece, earlier):
    arrays = [piece, *earlier]
    return pl.pallas_call(
        pass_kernel,
        in_specs=[pl.BlockSpec(memory_space=pl.ANY)] * len(arrays),
        out_specs=[pl.BlockSpec(memory_space=pl.ANY)] * len(arrays),
        out_shape=[jax.ShapeDtypeStruct(v.shape, v.dtype) for v in arrays],
        input_output_aliases={k: k for k in range(len(arrays))},
        cost_estimate=pl.CostEstimate(
            flops=20_000_000_000, bytes_accessed=100_000_000, transcendentals=0
        ),
        name="await_piece",
    )(*arrays)


def last_kernel(kept, third, second, first, out):
    @pl.when(pl.program_id(0) == 0)
    def _():
        wide = first.shape[1]
        out[:, :wide] = (kept[:, :wide] + first[...].astype(F32)).astype(BF)
        out[:, wide:] = (kept[:, wide:] + second[...].astype(F32)).astype(BF)

    @pl.when(pl.program_id(0) == 1)
    def _():
        out[...] = (kept[...] + third[...].astype(F32)).astype(BF)


def last_sums(kept, third, second, first):
    rows, wide = third.shape
    return pl.pallas_call(
        last_kernel,
        grid=(2,),
        in_specs=[
            pl.BlockSpec((rows, wide), lambda j: (0, j)),
            pl.BlockSpec((rows, wide), lambda j: (0, 0)),
            pl.BlockSpec(second.shape, lambda j: (0, 0)),
            pl.BlockSpec(first.shape, lambda j: (0, 0)),
        ],
        out_specs=pl.BlockSpec((rows, wide), lambda j: (0, j)),
        out_shape=jax.ShapeDtypeStruct(kept.shape, BF),
        compiler_params=pltpu.CompilerParams(vmem_limit_bytes=VMEM_LIMIT),
        name="last_sums",
    )(kept, third, second, first)


def per_device(
    seq_count,
    ssm_input,
    gate_input,
    step_raw,
    decay_log,
    state_in,
    state_out,
    skip_gain,
    norm_gain,
    out_weight,
):
    tok = ssm_input.shape[0]
    heads = decay_log.shape[0]
    b = state_in.reshape(tok, N)
    c = state_out.reshape(tok, N)
    give, wk, aux = give_states(step_raw.T, decay_log.reshape(1, heads), ssm_input, b)
    keep = keep_states(wk, ssm_input, b)
    skip = jnp.repeat(skip_gain, P_SIZE).reshape(1, -1)
    local = within(aux, ssm_input, b, c, gate_input, skip)
    (own, lead), here, there = incoming_states(
        give, keep, seq_count, lambda got: lax.optimization_barrier((local, got))
    )

    me = lax.axis_index("head")
    order = jnp.stack([me ^ 3, me ^ 2, me ^ 1, me]).astype(jnp.int32)
    near = [(h, h ^ 1) for h in range(4)]
    far = [(h, h ^ 2) for h in range(4)]
    gain = norm_gain.reshape(1, -1)

    def paired(theirs, mine):
        return mine + lax.ppermute(theirs, "head", near).astype(F32)

    theirs, mine, normed = finish_project(
        order, 0, own, lead, c, here, there, gain, out_weight, PIECES[0][1], "finish_far"
    )
    sent = [paired(theirs, mine).astype(BF)]
    for piece in PIECES[1:]:
        sent.append(paired(*project_more(normed, out_weight, *piece)).astype(BF))
        normed, sent[0] = lax.optimization_barrier((normed, sent[0]))
    order, sent[0] = lax.optimization_barrier((order, sent[0]))
    theirs, mine, _ = finish_project(
        order, 2, own, lead, c, here, there, gain, out_weight, out_weight.shape[1], "finish_near"
    )
    kept = paired(theirs, mine)
    arrived = []
    for part in sent:
        arrived = await_piece(lax.ppermute(part, "head", far), arrived)
    return last_sums(kept, *arrived)


def solution(mesh):
    in_specs = (
        P("seq", "head"),
        P("seq", "head"),
        P("seq", "head"),
        P("head"),
        P("seq", "head", None),
        P("seq", "head", None),
        P("head"),
        P("head"),
        P("head", None),
    )
    out_specs = P(("seq", "head"), None)
    return jax.shard_map(
        functools.partial(per_device, mesh.shape["seq"]),
        mesh=mesh,
        in_specs=in_specs,
        out_specs=out_specs,
        check_vma=False,
    )
```

time: 94.9 us -> 84.1 us (0.89)
  blocking collectives: 17.6 us -> 0 us
  local copies, waits for them, and re-layouts: 5.65 us -> 17.7 us
  starting transfers between devices: 7.74 us -> 18.5 us
  Pallas kernels: 35.7 us -> 25.2 us
  waiting for transfers between devices: 23 us -> 18.3 us
    all_to_all x1 -> x0, blocking collectives: 17.6 us -> none  [incoming_states(): arrived = lax.all_to_all(msg, 'seq', 0, 0, tiled=True)]
    ppermute x3 -> x7, starting transfers between devices: 3.61 us -> 17.3 us  [the longest x2 9.11 us: incoming_states(): lax.ppermute(run, 'seq', [(s, s + distance) for s in range(count - distan...]
    unnamed x20 -> x46, local copies, waits for them, and re-layouts: 5.5 us -> 17.5 us
    pallas_call x8 -> x13, Pallas kernels: 29.9 us -> 19.4 us  [the longest x2 8.84 us: finish_project(): pl.pallas_call(finish_kernel, grid_spec=pltpu.PrefetchScalarGridSpec(num_...]
    ppermute x4, waiting for transfers between devices: 3.72 us -> 0.1 us  [paired(): return mine + lax.ppermute(theirs, 'head', near).astype(F32)]
    all_to_all x1 -> x0, starting transfers between devices: 3.41 us -> none  [incoming_states(): return lax.all_to_all(prefix(arrived), 'seq', 0, 0, tiled=True)]
    add x1, other arithmetic: 0.21 us -> 1.48 us  [paired(): return mine + lax.ppermute(theirs, 'head', near).astype(F32)]
    ppermute x3 -> x7, waiting for transfers between devices: 19.3 us -> 18.2 us  [the longest x3 10.4 us: per_device(): arrived = await_piece(lax.ppermute(part, 'head', far), arrived)]
  transfers between devices with their start and end apart: 8 -> 11, of which waited for: 5 -> 5; matrix products, arithmetic and copies ran while one was open for 2% -> 5% of each run, Pallas kernels for 11% -> 21%
where the time goes in v1:
time: 84.1 us; the launch traced here: 83.6 us
  Pallas kernels  25.2 us (30%)
  starting transfers between devices  18.5 us (22%)
  waiting for transfers between devices  18.3 us (22%)
  local copies, waits for them, and re-layouts  17.7 us (21%)
  other arithmetic  3.66 us (4%)
    unnamed x46, local copies, waits for them, and re-layouts  17.5 us
    ppermute x3, waiting for transfers between devices, per_device(): arrived = await_piece(lax.ppermute(part, 'head', far), arrived)  10.4 us
    ppermute x2, starting transfers between devices, incoming_states(): lax.ppermute(run, 'seq', [(s, s + distance) for s in range(count - distan...  9.11 us
    pallas_call x2, Pallas kernels, finish_project(): pl.pallas_call(finish_kernel, grid_spec=pltpu.PrefetchScalarGridSpec(num_...  8.84 us
    pallas_call x1, Pallas kernels, within(): pl.pallas_call(within_kernel, grid=(channels // width,), in_specs=[pl.Blo...  5.81 us
    pallas_call x2, Pallas kernels, project_more(): pl.pallas_call(functools.partial(more_kernel, start), in_specs=[pl.BlockS...  4.31 us
    ppermute x3, starting transfers between devices, per_device(): arrived = await_piece(lax.ppermute(part, 'head', far), arrived)  3.67 us
    ppermute x1, waiting for transfers between devices, incoming_states(): return (hold, mine, lax.ppermute(theirs, 'seq', pair))  3.42 us
  transfers between devices with their start and end apart: 11, of which 5 were waited for; matrix products, arithmetic and copies ran while one was open for 5% of the time, Pallas kernels for 21%

profile of v1, /device:TPU:0, one launch (start us, length us, event | category | flops | bytes accessed | tf_op | source)
XLA Modules:
  0.0 83.6 jit_solution(6821863891197476307)
XLA Ops:
  0.0 2.9 %give_states.1 = (bf16[528,128]{1,0:T(8,128)(2,1)}, bf16[32,640]{1,0:T(8,128)(2,1)}, f32[48,512]{1,0:T(8,128)}) custom-call(f32[16,512]{1,0:T(8,128)} %bitcast.21, f32[1,16]{1,0:T(1,128)} %bitcast.22, f32[512,1024]{1,0:T(8,128)} %x.3, f32[512,128]{1,0:T(8,128)} %bitcast.16), custom_call_target="tpu_custom_call" | custom-call | flops 200000000 | bytes 1500000 | tf_op jit(solution)/shard_map/give_states/pallas_call | solution.py:155
  2.9 3.0 %collective-permute-start = (bf16[528,128]{1,0:T(8,128)(2,1)}, bf16[528,128]{1,0:T(8,128)(2,1)S(1)}, u32[]{:S(2)}, u32[]{:S(2)}) collective-permute-start(bf16[528,128]{1,0:T(8,128)(2,1)} %get-tuple-element.38), channel_id=1, source_target_pairs={{0,4},{4,0},{8,12},{12,8},{16,20},{20,16},{24,28},{28,24},{1,5},{5... | collective-permute-start | bytes 405512 | tf_op jit(solution)/shard_map/ppermute | solution.py:249
  7.7 2.0 %collective-permute-done.come = bf16[528,128]{1,0:T(8,128)(2,1)S(1)} collective-permute-done((bf16[528,128]{1,0:T(8,128)(2,1)}, bf16[528,128]{1,0:T(8,128)(2,1)S(1)}, u32[]{:S(2)}, u32[]{:S(2)}) %collective-permute-start) | collective-permute-done | bytes 135200 | tf_op jit(solution)/shard_map/ppermute | solution.py:249
  9.8 3.7 %collective-permute-start.1 = (bf16[528,128]{1,0:T(8,128)(2,1)S(1)}, bf16[528,128]{1,0:T(8,128)(2,1)S(1)}, u32[]{:S(2)}, u32[]{:S(2)}) collective-permute-start(bf16[528,128]{1,0:T(8,128)(2,1)S(1)} %join_pair.1.later), channel_id=1, source_target_pairs={{0,8},{4,12},{8,16},{12,20},{16,24},{20,28},{1,9},{5,13},{9,17},{1... | collective-permute-start | bytes 405512 | tf_op jit(solution)/shard_map/ppermute | solution.py:253
  13.7 2.4 %collective-permute-done.1.earlier.last = bf16[528,128]{1,0:T(8,128)(2,1)S(1)} collective-permute-done((bf16[528,128]{1,0:T(8,128)(2,1)S(1)}, bf16[528,128]{1,0:T(8,128)(2,1)S(1)}, u32[]{:S(2)}, u32[]{:S(2)}) %collective-permute-start.1) | collective-permute-done | bytes 135200 | tf_op jit(solution)/shard_map/ppermute | solution.py:253
  16.1 5.4 %collective-permute-start.2 = (bf16[528,128]{1,0:T(8,128)(2,1)S(1)}, bf16[528,128]{1,0:T(8,128)(2,1)S(1)}, u32[]{:S(2)}, u32[]{:S(2)}) collective-permute-start(bf16[528,128]{1,0:T(8,128)(2,1)S(1)} %join_run.1), channel_id=1, source_target_pairs={{0,16},{4,20},{8,24},{12,28},{1,17},{5,21},{9,25},{13,29},{2,18},{... | collective-permute-start | bytes 405512 | tf_op jit(solution)/shard_map/ppermute | solution.py:253
  21.6 1.6 %copy-done.6 = f32[512,1024]{1,0:T(8,128)S(1)} copy-done((f32[512,1024]{1,0:T(8,128)S(1)}, f32[512,1024]{1,0:T(8,128)}, u32[]{:S(2)}) %copy-start.6) | copy-done | bytes 2097176
  23.1 1.2 %copy-done.17 = bf16[512,1024]{1,0:T(8,128)(2,1)S(1)} copy-done((bf16[512,1024]{1,0:T(8,128)(2,1)S(1)}, bf16[512,1024]{1,0:T(8,128)(2,1)}, u32[]{:S(2)}) %copy-start.17) | copy-done | bytes 1048600
  24.4 5.8 %within.1 = (f32[512,1024]{1,0:T(8,128)S(1)}, f32[512,1024]{1,0:T(8,128)S(1)}) custom-call(f32[48,512]{1,0:T(8,128)S(1)} %copy-done.18, f32[512,1024]{1,0:T(8,128)S(1)} %copy-done.6, f32[512,128]{1,0:T(8,128)S(1)} %bitcast.18, f32[512,128]{1,0:T(8,128)S(1)} %bitcast.11, bf16[512,1024]{1,0:T(8,128)(2,1)S(1)} %copy-done.17, f32[1,1024]{1,0:T(1,128)S(1)} %reshape_reshape.3.skip_ref), custom_call_target="tpu_custom_call" | custom-call | flops 2000000000 | bytes 5000000 | tf_op jit(solution)/shard_map/within/pallas_call | solution.py:338
  30.2 1.3 %copy-done.2 = f32[512,1024]{1,0:T(8,128)} copy-done((f32[512,1024]{1,0:T(8,128)}, f32[512,1024]{1,0:T(8,128)S(1)}, u32[]{:S(2)}) %copy-start.2) | copy-done | bytes 2097176
  31.6 1.5 %collective-permute-start.3 = (bf16[512,128]{1,0:T(8,128)(2,1)S(1)}, bf16[512,128]{1,0:T(8,128)(2,1)S(1)}, u32[]{:S(2)}, u32[]{:S(2)}) collective-permute-start(bf16[512,128]{1,0:T(8,128)(2,1)S(1)} %get-tuple-element.43), channel_id=1, source_target_pairs={{0,4},{4,0},{8,12},{12,8},{16,20},{20,16},{24,28},{28,24},{1,5},{5... | collective-permute-start | bytes 393224 | tf_op jit(solution)/shard_map/ppermute | solution.py:262
  33.2 3.4 %collective-permute-done.3.there = bf16[512,128]{1,0:T(8,128)(2,1)S(1)} collective-permute-done((bf16[512,128]{1,0:T(8,128)(2,1)S(1)}, bf16[512,128]{1,0:T(8,128)(2,1)S(1)}, u32[]{:S(2)}, u32[]{:S(2)}) %collective-permute-start.3) | collective-permute-done | bytes 131104 | tf_op jit(solution)/shard_map/ppermute | solution.py:262
  36.7 3.4 %copy-done = bf16[1024,4096]{1,0:T(8,128)(2,1)S(1)} copy-done((bf16[1024,4096]{1,0:T(8,128)(2,1)S(1)}, bf16[1024,4096]{1,0:T(8,128)(2,1)}, u32[]{:S(2)}) %copy-start) | copy-done | bytes 8388632
  40.1 1.6 %copy-done.3 = f32[512,1024]{1,0:T(8,128)S(1)} copy-done((f32[512,1024]{1,0:T(8,128)S(1)}, f32[512,1024]{1,0:T(8,128)}, u32[]{:S(2)}) %copy-start.3) | copy-done | bytes 2097176
  41.7 2.2 %finish_far.1 = (bf16[128,1024]{1,0:T(8,128)(2,1)S(1)}, f32[128,1024]{1,0:T(8,128)S(1)}, bf16[256,1024]{1,0:T(8,128)(2,1)S(1)}) custom-call(s32[4]{0:T(128)S(1)} %pad_add_fusion.order, f32[512,1024]{1,0:T(8,128)S(1)} %get-tuple-element.39.o0.o1, f32[512,1024]{1,0:T(8,128)S(1)} %get-tuple-element.39.o0.o1, f32[512,1024]{1,0:T(8,128)S(1)} %copy-done.3, ...), custom_call_target="tpu_custom_call" | custom-call | flops 536870912 | bytes 2097152 | tf_op jit(solution)/shard_map/finish_far/pallas_call | solution.py:421
  44.0 3.4 %copy-done.1 = bf16[1024,4096]{1,0:T(8,128)(2,1)S(1)} copy-done((bf16[1024,4096]{1,0:T(8,128)(2,1)S(1)}, bf16[1024,4096]{1,0:T(8,128)(2,1)}, u32[]{:S(2)}) %copy-start.1) | copy-done | bytes 8388632
  49.2 1.6 %collective-permute-start.10 = (bf16[128,1024]{1,0:T(8,128)(2,1)S(1)}, bf16[128,1024]{1,0:T(8,128)(2,1)}, u32[]{:S(2)}, u32[]{:S(2)}) collective-permute-start(bf16[128,1024]{1,0:T(8,128)(2,1)S(1)} %add_convert_fusion.2), channel_id=1, source_target_pairs={{0,2},{1,3},{2,0},{3,1},{4,6},{5,7},{6,4},{7,5},{8,10},{9,11},{10,... | collective-permute-start | bytes 786440 | tf_op jit(solution)/shard_map/ppermute | solution.py:589
  52.6 3.1 %project_more.2 = (bf16[128,2048]{1,0:T(8,128)(2,1)}, f32[128,2048]{1,0:T(8,128)S(1)}) custom-call(bf16[256,1024]{1,0:T(8,128)(2,1)S(1)} %get-tuple-element.51.normed, bf16[1024,4096]{1,0:T(8,128)(2,1)S(1)} %copy-done.1), custom_call_target="tpu_custom_call" | custom-call | flops 1073741824 | bytes 4194304 | tf_op jit(solution)/shard_map/project_more/pallas_call | solution.py:472
  55.9 6.6 %finish_near.1 = (bf16[128,4096]{1,0:T(8,128)(2,1)}, f32[128,4096]{1,0:T(8,128)S(1)}, bf16[256,1024]{1,0:T(8,128)(2,1)}) custom-call(s32[4]{0:T(128)S(1)} %pad_add_fusion.order, f32[512,1024]{1,0:T(8,128)S(1)} %get-tuple-element.39.o0.o1, f32[512,1024]{1,0:T(8,128)S(1)} %get-tuple-element.39.o0.o1, f32[512,1024]{1,0:T(8,128)S(1)} %copy-done.4, ...), custom_call_target="tpu_custom_call" | custom-call | flops 2147483648 | bytes 8388608 | tf_op jit(solution)/shard_map/finish_near/pallas_call | solution.py:421
  62.5 1.3 %copy-done.8 = f32[128,4096]{1,0:T(8,128)} copy-done((f32[128,4096]{1,0:T(8,128)}, f32[128,4096]{1,0:T(8,128)S(1)}, u32[]{:S(2)}) %copy-start.8) | copy-done | bytes 2097176
  64.3 1.3 %add_convert_fusion = bf16[128,2048]{1,0:T(8,128)(2,1)S(1)} fusion(f32[128,2048]{1,0:T(8,128)S(1)} %get-tuple-element.52, bf16[128,2048]{1,0:T(8,128)(2,1)} %collective-permute-done.6), kind=kLoop, calls=%fused_computation.1 | loop fusion | flops 786432 | bytes 2097152 | tf_op jit(solution)/shard_map/convert_element_type | solution.py:580
  67.8 1.5 %convert_add_fusion.kept = f32[128,4096]{1,0:T(8,128)S(1)} fusion(f32[128,4096]{1,0:T(8,128)S(1)} %copy-done.9, bf16[128,4096]{1,0:T(8,128)(2,1)} %copy-done.19), kind=kLoop, calls=%fused_computation | loop fusion | flops 1048576 | bytes 5242880 | tf_op jit(solution)/shard_map/add | solution.py:573
  69.3 10.4 %collective-permute-done.7.refs_0_ = bf16[128,2048]{1,0:T(8,128)(2,1)S(1)} collective-permute-done((bf16[128,2048]{1,0:T(8,128)(2,1)S(1)}, bf16[128,2048]{1,0:T(8,128)(2,1)S(1)}, u32[]{:S(2)}, u32[]{:S(2)}) %collective-permute-start.7) | collective-permute-done | bytes 524320 | tf_op jit(solution)/shard_map/ppermute | solution.py:589
  81.5 2.2 %last_sums.1 = bf16[128,4096]{1,0:T(8,128)(2,1)} custom-call(f32[128,4096]{1,0:T(8,128)S(1)} %convert_add_fusion.kept, bf16[128,2048]{1,0:T(8,128)(2,1)S(1)} %copy-done.14, bf16[128,1024]{1,0:T(8,128)(2,1)} %get-tuple-element.60.second, bf16[128,1024]{1,0:T(8,128)(2,1)} %get-tuple-element.61.first), custom_call_target="tpu_custom_call" | custom-call | tf_op jit(solution)/shard_map/last_sums/pallas_call | solution.py:526
  (66 shorter events, 10.4 us)
Async XLA Ops:
  0.0 5.9 %copy-start.5 = (f32[512,1024]{1,0:T(8,128)S(1)}, f32[512,1024]{1,0:T(8,128)}, u32[]{:S(2)}) copy-start(f32[512,1024]{1,0:T(8,128)} %x.3) | copy-start | bytes 6291460
  0.0 5.9 %copy-start.10 = (f32[512,1,128]{2,1,0:T(1,128)S(1)}, f32[512,1,128]{2,1,0:T(1,128)}, u32[]{:S(2)}) copy-start(f32[512,1,128]{2,1,0:T(1,128)} %param.13) | copy-start | bytes 786436
  0.0 13.5 %copy-start.20 = (f32[16]{0:T(128)S(1)}, f32[16]{0:T(128)}, u32[]{:S(2)}) copy-start(f32[16]{0:T(128)} %param.15) | copy-start | bytes 196
  2.9 18.6 %copy-start.7 = (f32[512,1,128]{2,1,0:T(1,128)S(1)}, f32[512,1,128]{2,1,0:T(1,128)}, u32[]{:S(2)}) copy-start(f32[512,1,128]{2,1,0:T(1,128)} %param.14) | copy-start | bytes 786436
  2.9 6.8 %collective-permute-start = (bf16[528,128]{1,0:T(8,128)(2,1)}, bf16[528,128]{1,0:T(8,128)(2,1)S(1)}, u32[]{:S(2)}, u32[]{:S(2)}) collective-permute-start(bf16[528,128]{1,0:T(8,128)(2,1)} %get-tuple-element.38), channel_id=1, source_target_pairs={{0,4},{4,0},{8,12},{12,8},{16,20},{20,16},{24,28},{28,24},{1,5},{5... | collective-permute-start | bytes 405512 | tf_op jit(solution)/shard_map/ppermute | solution.py:249
  6.7 14.8 %copy-start.18 = (f32[48,512]{1,0:T(8,128)S(1)}, f32[48,512]{1,0:T(8,128)}, u32[]{:S(2)}) copy-start(f32[48,512]{1,0:T(8,128)} %get-tuple-element.34.aux_ref) | copy-start | bytes 294916
  9.8 6.3 %collective-permute-start.1 = (bf16[528,128]{1,0:T(8,128)(2,1)S(1)}, bf16[528,128]{1,0:T(8,128)(2,1)S(1)}, u32[]{:S(2)}, u32[]{:S(2)}) collective-permute-start(bf16[528,128]{1,0:T(8,128)(2,1)S(1)} %join_pair.1.later), channel_id=1, source_target_pairs={{0,8},{4,12},{8,16},{12,20},{16,24},{20,28},{1,9},{5,13},{9,17},{1... | collective-permute-start | bytes 405512 | tf_op jit(solution)/shard_map/ppermute | solution.py:253
  16.1 15.4 %collective-permute-start.2 = (bf16[528,128]{1,0:T(8,128)(2,1)S(1)}, bf16[528,128]{1,0:T(8,128)(2,1)S(1)}, u32[]{:S(2)}, u32[]{:S(2)}) collective-permute-start(bf16[528,128]{1,0:T(8,128)(2,1)S(1)} %join_run.1), channel_id=1, source_target_pairs={{0,16},{4,20},{8,24},{12,28},{1,17},{5,21},{9,25},{13,29},{2,18},{... | collective-permute-start | bytes 405512 | tf_op jit(solution)/shard_map/ppermute | solution.py:253
  24.4 12.3 %copy-start.16 = (f32[1024]{0:T(1024)S(1)}, f32[1024]{0:T(1024)}, u32[]{:S(2)}) copy-start(f32[1024]{0:T(1024)} %param.16) | copy-start | bytes 12292
  31.6 5.0 %collective-permute-start.3 = (bf16[512,128]{1,0:T(8,128)(2,1)S(1)}, bf16[512,128]{1,0:T(8,128)(2,1)S(1)}, u32[]{:S(2)}, u32[]{:S(2)}) collective-permute-start(bf16[512,128]{1,0:T(8,128)(2,1)S(1)} %get-tuple-element.43), channel_id=1, source_target_pairs={{0,4},{4,0},{8,12},{12,8},{16,20},{20,16},{24,28},{28,24},{1,5},{5... | collective-permute-start | bytes 393224 | tf_op jit(solution)/shard_map/ppermute | solution.py:262
  36.7 7.2 %copy-start.11 = (bf16[512,128]{1,0:T(8,128)(2,1)}, bf16[512,128]{1,0:T(8,128)(2,1)S(1)}, u32[]{:S(2)}) copy-start(bf16[512,128]{1,0:T(8,128)(2,1)S(1)} %collective-permute-done.3.there) | copy-start | bytes 393220
  36.7 3.4 %copy-start = (bf16[1024,4096]{1,0:T(8,128)(2,1)S(1)}, bf16[1024,4096]{1,0:T(8,128)(2,1)}, u32[]{:S(2)}) copy-start(bf16[1024,4096]{1,0:T(8,128)(2,1)} %w.7) | copy-start | bytes 25165828
  43.9 5.2 %collective-permute-start.4 = (bf16[128,1024]{1,0:T(8,128)(2,1)S(1)}, bf16[128,1024]{1,0:T(8,128)(2,1)S(1)}, u32[]{:S(2)}, u32[]{:S(2)}) collective-permute-start(bf16[128,1024]{1,0:T(8,128)(2,1)S(1)} %get-tuple-element.46), channel_id=1, source_target_pairs={{0,1},{1,0},{2,3},{3,2},{4,5},{5,4},{6,7},{7,6},{8,9},{9,8},{10,11... | collective-permute-start | bytes 786440 | tf_op jit(solution)/shard_map/ppermute | solution.py:573
  47.4 8.5 %slice-start = ((s8[8388608]{0:T(1024)(128)(4,1)}), s8[4194304]{0:T(1024)(128)(4,1)S(1)}, s32[]{:S(2)}) async-start(s8[8388608]{0:T(1024)(128)(4,1)} %bitcast.9), calls=%async_computation | async-start | bytes 8388608
  48.6 2.2 %collective-permute-start.8 = (bf16[128,1024]{1,0:T(8,128)(2,1)S(1)}, bf16[128,1024]{1,0:T(8,128)(2,1)S(1)}, u32[]{:S(2)}, u32[]{:S(2)}) collective-permute-start(bf16[128,1024]{1,0:T(8,128)(2,1)S(1)} %get-tuple-element.55), channel_id=1, source_target_pairs={{0,1},{1,0},{2,3},{3,2},{4,5},{5,4},{6,7},{7,6},{8,9},{9,8},{10,11... | collective-permute-start | bytes 786440 | tf_op jit(solution)/shard_map/ppermute | solution.py:573
  49.2 6.7 %slice-start.1 = ((s8[8388608]{0:T(1024)(128)(4,1)}), s8[4194304]{0:T(1024)(128)(4,1)S(1)}, s32[]{:S(2)}) async-start(s8[8388608]{0:T(1024)(128)(4,1)} %bitcast.9), calls=%async_computation.1 | async-start | bytes 8388608
  49.2 15.1 %collective-permute-start.10 = (bf16[128,1024]{1,0:T(8,128)(2,1)S(1)}, bf16[128,1024]{1,0:T(8,128)(2,1)}, u32[]{:S(2)}, u32[]{:S(2)}) collective-permute-start(bf16[128,1024]{1,0:T(8,128)(2,1)S(1)} %add_convert_fusion.2), channel_id=1, source_target_pairs={{0,2},{1,3},{2,0},{3,1},{4,6},{5,7},{6,4},{7,5},{8,10},{9,11},{10,... | collective-permute-start | bytes 786440 | tf_op jit(solution)/shard_map/ppermute | solution.py:589
  51.5 4.3 %copy-start.4 = (f32[512,1024]{1,0:T(8,128)S(1)}, f32[512,1024]{1,0:T(8,128)}, u32[]{:S(2)}) copy-start(f32[512,1024]{1,0:T(8,128)} %copy-done.2) | copy-start | bytes 6291460
  51.5 4.3 %copy-start.12 = (bf16[512,128]{1,0:T(8,128)(2,1)S(1)}, bf16[512,128]{1,0:T(8,128)(2,1)}, u32[]{:S(2)}) copy-start(bf16[512,128]{1,0:T(8,128)(2,1)} %copy-done.11) | copy-start | bytes 393220
  51.5 12.8 %collective-permute-start.9 = (bf16[128,1024]{1,0:T(8,128)(2,1)}, bf16[128,1024]{1,0:T(8,128)(2,1)}, u32[]{:S(2)}, u32[]{:S(2)}) collective-permute-start(bf16[128,1024]{1,0:T(8,128)(2,1)} %add_convert_fusion.1), channel_id=1, source_target_pairs={{0,2},{1,3},{2,0},{3,1},{4,6},{5,7},{6,4},{7,5},{8,10},{9,11},{10,... | collective-permute-start | bytes 786440 | tf_op jit(solution)/shard_map/ppermute | solution.py:589
  55.7 8.6 %collective-permute-start.6 = (bf16[128,2048]{1,0:T(8,128)(2,1)}, bf16[128,2048]{1,0:T(8,128)(2,1)}, u32[]{:S(2)}, u32[]{:S(2)}) collective-permute-start(bf16[128,2048]{1,0:T(8,128)(2,1)} %get-tuple-element.53), channel_id=1, source_target_pairs={{0,1},{1,0},{2,3},{3,2},{4,5},{5,4},{6,7},{7,6},{8,9},{9,8},{10,11... | collective-permute-start | bytes 1572872 | tf_op jit(solution)/shard_map/ppermute | solution.py:573
  63.9 2.9 %collective-permute-start.5 = (bf16[128,4096]{1,0:T(8,128)(2,1)}, bf16[128,4096]{1,0:T(8,128)(2,1)S(1)}, u32[]{:S(2)}, u32[]{:S(2)}) collective-permute-start(bf16[128,4096]{1,0:T(8,128)(2,1)} %get-tuple-element.50), channel_id=1, source_target_pairs={{0,1},{1,0},{2,3},{3,2},{4,5},{5,4},{6,7},{7,6},{8,9},{9,8},{10,11... | collective-permute-start | bytes 3145736 | tf_op jit(solution)/shard_map/ppermute | solution.py:573
  64.3 3.5 %copy-start.9 = (f32[128,4096]{1,0:T(8,128)S(1)}, f32[128,4096]{1,0:T(8,128)}, u32[]{:S(2)}) copy-start(f32[128,4096]{1,0:T(8,128)} %copy-done.8) | copy-start | bytes 6291460
  65.6 14.0 %collective-permute-start.7 = (bf16[128,2048]{1,0:T(8,128)(2,1)S(1)}, bf16[128,2048]{1,0:T(8,128)(2,1)S(1)}, u32[]{:S(2)}, u32[]{:S(2)}) collective-permute-start(bf16[128,2048]{1,0:T(8,128)(2,1)S(1)} %add_convert_fusion), channel_id=1, source_target_pairs={{0,2},{1,3},{2,0},{3,1},{4,6},{5,7},{6,4},{7,5},{8,10},{9,11},{10,... | collective-permute-start | bytes 1572872 | tf_op jit(solution)/shard_map/ppermute | solution.py:589
  (10 other events, 14.1 us)
